TPU v7x, 512 devices: a whole 4x8x8 slice. The times are simulated.
512 devices in a mesh: rep: 16 (over y, x_lo), fsdp: 8 (over z), tp: 4 (over x_hi, core).
Axes of the slice: x: 4 (x_hi: 2, x_lo: 2; x = x_hi * 2 + x_lo), y: 8, z: 8, core: 2. Of those that a mesh axis runs over, the one named last changes fastest.
Arguments:
- grad_parts: bfloat16 [8, 2, 8192, 1024], P('fsdp', None, 'rep', 'tp'), may hold values from -4 to 4
- master_weight: float32 [2, 8192, 1024], P(None, ('rep', 'fsdp'), 'tp'), may hold values from -0.0625 to 0.0625
- moment_one: float32 [2, 8192, 1024], P(None, ('rep', 'fsdp'), 'tp'), may hold values from -4 to 4
- moment_two: float32 [2, 8192, 1024], P(None, ('rep', 'fsdp'), 'tp'), may hold values from 0.1 to 2
- layer_inputs: bfloat16 [6144, 4, 8192], P(('rep', 'fsdp'), None, 'tp'), may hold values from -6 to 6
- queries: bfloat16 [6144, 4, 8192], P(('rep', 'fsdp'), None, 'tp'), may hold values from -105 to 105
- kv_cache: bfloat16 [6144, 24, 2, 1024], P(('rep', 'fsdp'), None, None, 'tp'), may hold values from -4 to 4
- lengths: int32 [6144], P(('rep', 'fsdp')), may hold values from 2 to 24
Outputs:
- new_master: float32 [2, 8192, 1024], P(None, ('rep', 'fsdp'), 'tp')
- new_moment_one: float32 [2, 8192, 1024], P(None, ('rep', 'fsdp'), 'tp')
- new_moment_two: float32 [2, 8192, 1024], P(None, ('rep', 'fsdp'), 'tp')
- context: bfloat16 [6144, 4, 8192], P(('rep', 'fsdp'), None, 'tp')
Inputs may be any that keep to these rules, and one draw needn't show every extreme that they name: lengths[r] is the number of valid cached positions of row r, at most 24.
All inputs are finite; a program needn't handle non-finite values.
Results may differ from a plain program's by a relative error of at most 0.0065.
Values may be sent and summed in bfloat16 or wider, within the bound.
No kernel may reach another device: no remote copies, remote signals or barrier semaphores. Data moves between devices by JAX's collectives and lax.ppermute only.
A program may use at most 64 MiB of HBM per device.

v0:
```python
import jax
import jax.numpy as jnp
from jax import lax
from jax.sharding import Mesh
from jax.sharding import PartitionSpec as P

HD = 128
REP_FSDP = ("rep_0", "rep_1", "fsdp")
REP = ("rep_0", "rep_1")
beta_one = 0.9
beta_two = 0.95
learning_rate = 0.001
weight_decay = 0.1
epsilon = 1e-08
first_bias = 1.0 - 0.9**10
second_bias = 1.0 - 0.95**10


def split_up(x, dim, size):
    dims = x.shape
    parts = x.reshape(*dims[:dim], size, dims[dim] // size, *dims[dim + 1 :])
    return jnp.moveaxis(parts, dim, 0)


def sent_and_summed(x, axis, dim):
    size = lax.axis_size(axis)
    parts = lax.all_to_all(split_up(x, dim, size), axis, 0, 0, tiled=True)
    return jnp.sum(parts.astype(jnp.float32), axis=0)


def in_order(parts, dim):
    dims = list(parts.shape[1:])
    dims[dim] *= parts.shape[0]
    return jnp.moveaxis(parts, 0, dim).reshape(dims)


def all_blocks(x, axes, turns):
    parts = x
    for k in turns:
        parts = lax.all_gather(parts, axes[k])
    done = turns[::-1]
    back = [done.index(k) for k in range(len(axes))]
    parts = parts.transpose(*back, *range(len(axes), parts.ndim))
    return parts.reshape(-1, *x.shape)


def whole_of(x, axes, turns, dim):
    return in_order(all_blocks(x, axes, turns), dim)


def adamw_update(gradient, master, moment_one, moment_two):
    new_one = beta_one * moment_one + (1.0 - beta_one) * gradient
    new_two = beta_two * moment_two + (1.0 - beta_two) * gradient * gradient
    update = new_one / first_bias / (jnp.sqrt(new_two / second_bias) + epsilon)
    new_master = master - learning_rate * (update + weight_decay * master)
    return (new_one, new_two, new_master)


def attend(queries, kv_cache, fresh_keys, fresh_values, lengths):
    row_count = queries.shape[0]
    step_count = queries.shape[1]
    kv_heads = fresh_keys.shape[2]
    cache_len = kv_cache.shape[1]
    grouped = queries.reshape(row_count, step_count, kv_heads, -1, HD)
    cached_keys = kv_cache[:, :, 0].reshape(row_count, cache_len, kv_heads, HD)
    cached_values = kv_cache[:, :, 1].reshape(row_count, cache_len, kv_heads, HD)
    scaling = 1.0 / jnp.sqrt(jnp.float32(HD))
    cached_scores = (
        jnp.einsum("rsgqd,rcgd->rsgqc", grouped, cached_keys, preferred_element_type=jnp.float32)
        * scaling
    )
    fresh_scores = (
        jnp.einsum("rsgqd,rugd->rsgqu", grouped, fresh_keys, preferred_element_type=jnp.float32)
        * scaling
    )
    valid_old = jnp.arange(cache_len, dtype=jnp.int32)[None, :] < lengths[:, None]
    valid_old = valid_old[:, None, None, None, :]
    steps_index = jnp.arange(step_count, dtype=jnp.int32)
    valid_new = (steps_index[None, :] <= steps_index[:, None])[None, :, None, None, :]
    scores = jnp.concatenate(
        [
            jnp.where(valid_old, cached_scores, -jnp.inf),
            jnp.where(valid_new, fresh_scores, -jnp.inf),
        ],
        axis=-1,
    )
    row_max = jnp.max(scores, axis=-1, keepdims=True)
    exponent = jnp.exp(scores - row_max)
    weights = (exponent / jnp.sum(exponent, axis=-1, keepdims=True)).astype(jnp.bfloat16)
    output = jnp.einsum(
        "rsgqc,rcgd->rsgqd",
        weights[..., :cache_len],
        cached_values,
        preferred_element_type=jnp.float32,
    )
    output = output + jnp.einsum(
        "rsgqu,rugd->rsgqd",
        weights[..., cache_len:],
        fresh_values,
        preferred_element_type=jnp.float32,
    )
    return output.astype(jnp.bfloat16).reshape(row_count, step_count, -1)


def on_device(
    grad_parts, master_weight, moment_one, moment_two, layer_inputs, queries, kv_cache, lengths
):
    gradient = sent_and_summed(grad_parts[0].astype(jnp.float32).astype(jnp.bfloat16), "fsdp", 1)
    new_one, new_two, new_master = adamw_update(gradient, master_weight, moment_one, moment_two)
    rollout_weight = new_master.astype(jnp.bfloat16)
    row_count = layer_inputs.shape[0]
    step_count = layer_inputs.shape[1]
    gathered = lax.all_gather(layer_inputs, "tp", axis=2, tiled=True)
    flattened = gathered.reshape(row_count * step_count, gathered.shape[2])
    projected = jnp.einsum(
        "td,kdc->ktc",
        flattened,
        whole_of(rollout_weight, REP_FSDP, (1, 0, 2), 1),
        preferred_element_type=jnp.float32,
    )
    fresh_pair = projected.astype(jnp.bfloat16).reshape(2, row_count, step_count, -1, HD)
    context = attend(queries, kv_cache, fresh_pair[0], fresh_pair[1], lengths)
    return (new_master, new_one, new_two, context)


def solution(mesh):
    finer = Mesh(
        mesh.devices.reshape(8, 2, mesh.shape["fsdp"], mesh.shape["tp"]),
        ("rep_0", "rep_1", "fsdp", "tp"),
    )
    return jax.shard_map(
        on_device,
        mesh=finer,
        in_specs=(
            P("fsdp", None, REP, "tp"),
            P(None, REP_FSDP, "tp"),
            P(None, REP_FSDP, "tp"),
            P(None, REP_FSDP, "tp"),
            P(REP_FSDP, None, "tp"),
            P(REP_FSDP, None, "tp"),
            P(REP_FSDP, None, None, "tp"),
            P(REP_FSDP),
        ),
        out_specs=(
            P(None, REP_FSDP, "tp"),
            P(None, REP_FSDP, "tp"),
            P(None, REP_FSDP, "tp"),
            P(REP_FSDP, None, "tp"),
        ),
        check_vma=False,
    )
```

profile of v0, /device:TPU:1, one launch (start us, length us, event | category | flops | bytes accessed | tf_op | source)
XLA Modules:
  0.0 261.9 jit_solution(16892887311878744765)
XLA Ops:
  7.2 0.0 copy-start.6
  7.2 0.0 copy-start.7
  7.2 0.0 copy-start.5
  7.2 0.0 all-gather.9.cloned.1.call-start
  7.2 1.2 copy.94
  8.4 26.7 %all_to_all.5 = bf16[8,2,64,256]{3,2,1,0:T(8,128)(2,1)S(1)} all-to-all(bf16[8,2,64,256]{3,2,1,0:T(8,128)(2,1)S(1)} %copy.94), channel_id=1, replica_groups=mesh['rep_0'=8,'rep_1'=2,'fsdp'=8,'tp'=4] {'fsdp'}, dimensions={0} | all-to-all | bytes 1048576 | tf_op jit(solution)/shard_map/all_to_all | solution.py:27
  35.1 0.1 convert_reduce_fusion
  35.2 0.0 copy-done.6
  35.2 0.0 copy-done.7
  35.2 0.0 copy-done.5
  35.2 0.0 copy-start.3
  35.2 0.8 fusion.16
  36.0 3.9 %all-gather = bf16[4,64,256]{2,1,0:T(8,128)(2,1)} all-gather(bf16[2,64,256]{2,1,0:T(8,128)(2,1)S(1)} %get-tuple-element.36), channel_id=2, replica_groups=mesh['rep_0'=8,'rep_1'=2,'fsdp'=8,'tp'=4] {'rep_1'}, dimensions={0}, use_global_device_ids=true | all-gather | bytes 196608 | tf_op jit(solution)/shard_map/all_gather | solution.py:40
  39.9 0.0 all-gather.9.cloned.1.call-update
  39.9 0.0 copy-start.1
  39.9 0.0 all-gather.7.cloned.1.call-start
  40.0 0.7 all-gather.7.cloned.1.call-update
  40.7 0.0 all-gather.11.cloned.1.call-start
  40.7 35.4 %all-gather.9.cloned.1.call-done = bf16[16,2,64,256]{3,2,1,0:T(8,128)(2,1)} async-done(((bf16[2,2,64,256]{3,2,1,0:T(8,128)(2,1)}), bf16[16,2,64,256]{3,2,1,0:T(8,128)(2,1)}) %all-gather.9.cloned.1.call-update) | async-done | bytes 1048592 | tf_op jit(solution)/shard_map/all_gather | solution.py:40
  76.1 0.0 all-gather.11.cloned.1.call-update
  76.2 0.0 copy-done.3
  76.2 0.5 reshape.68
  76.7 0.0 copy-done.1
  76.7 4.9 %slice_reduce_fusion = (bf16[48,24,256]{2,1,0:T(8,128)(2,1)S(1)}, bf16[48,24,256]{2,1,0:T(8,128)(2,1)S(1)}) fusion(bf16[48,24,2,256]{3,2,1,0:T(2,128)(2,1)S(1)} %copy-done.1), kind=kLoop, calls=%fused_computation.6 | loop fusion | bytes 2359296 | tf_op jit(solution)/shard_map/slice | solution.py:66
  81.6 0.0 copy-start.8
  81.6 1.0 reshape_squeeze.6
  82.6 0.9 reshape_squeeze.7
  83.5 0.0 copy-done.8
  83.5 0.1 iota_compare_fusion
  83.6 1.7 fusion.19
  85.3 34.1 %all-gather.7.cloned.1.call-done = bf16[48,4,8192]{2,1,0:T(4,128)(2,1)} async-done(((bf16[48,4,2048]{2,1,0:T(4,128)(2,1)}), bf16[48,4,8192]{2,1,0:T(4,128)(2,1)}) %all-gather.7.cloned.1.call-update) | async-done | bytes 3145744 | tf_op jit(solution)/shard_map/all_gather | solution.py:113
  119.4 5.5 %reshape.77 = bf16[192,8192,1]{1,0,2:T(8,128)(2,1)} reshape(bf16[48,4,8192]{2,1,0:T(4,128)(2,1)} %all-gather.7.cloned.1.call-done) | data formatting | bytes 6291456 | tf_op jit(solution)/shard_map/reshape | solution.py:114
  124.9 93.3 %all-gather.11.cloned.1.call-done = bf16[64,2,2,64,256]{4,3,2,1,0:T(8,128)(2,1)} async-done(((bf16[8,2,2,64,256]{4,3,2,1,0:T(8,128)(2,1)}), bf16[64,2,2,64,256]{4,3,2,1,0:T(8,128)(2,1)}) %all-gather.11.cloned.1.call-update) | async-done | bytes 8388624 | tf_op jit(solution)/shard_map/all_gather | solution.py:40
  218.2 8.3 %copy.97 = bf16[8,2,8,2,64,256]{5,4,3,2,1,0:T(8,128)(2,1)} copy(bf16[8,2,8,2,64,256]{5,4,3,1,0,2:T(8,128)(2,1)} %bitcast.34) | data formatting | bytes 16777216 | tf_op jit(solution)/shard_map/transpose | solution.py:43
  226.5 0.0 copy-start.2
  226.5 8.4 %copy.98 = bf16[2,128,64,256]{3,2,1,0:T(8,128)(2,1)} copy(bf16[2,128,64,256]{3,2,0,1:T(8,128)(2,1)} %bitcast.33) | data formatting | bytes 16777216 | tf_op jit(solution)/shard_map/transpose | solution.py:34
  234.9 0.0 copy-done.2
  234.9 5.3 %fusion.2 = bf16[2,192,256]{2,1,0:T(8,128)(2,1)S(1)} fusion(bf16[192,8192,1]{1,0,2:T(8,128)(2,1)S(1)} %copy-done.2, bf16[2,8192,256]{2,1,0:T(8,128)(2,1)} %bitcast.35), kind=kOutput, calls=%fused_computation.9 | convolution fusion | flops 1610711040 | bytes 11730944 | tf_op jit(solution)/shard_map/td,kdc->ktc/dot_general | solution.py:115
  240.2 0.6 fusion.18
  240.9 3.5 %fusion.6 = f32[48,2,4,4,8]{4,2,3,1,0:T(4,128)S(1)} fusion(bf16[48,4,2,8,128]{4,3,2,1,0:T(8,128)(2,1)S(1)} %reshape.68, bf16[48,4,2,128,1]{3,2,1,0,4:T(2,128)(2,1)S(1)} %bitcast.42), kind=kOutput, calls=%fused_computation.14 | convolution fusion | flops 3145728 | bytes 933888 | tf_op jit(solution)/shard_map/rsgqd,rugd->rsgqu/dot_general | solution.py:73
  244.4 0.5 copy.101
  244.9 0.7 fusion.15
  245.6 0.1 copy.103
  245.8 2.4 copy.102
  248.2 0.1 reduce_max.22
  248.2 1.5 fusion.11
  249.7 0.0 copy-start.4
  249.7 2.2 divide_convert_fusion
  251.9 0.0 copy-done.4
  251.9 0.0 copy-start
  252.0 1.7 fusion.4
  253.7 0.0 copy-done
  253.7 0.4 fusion.1
  254.1 0.1 copy.122
  254.3 1.1 reshape.82
  (3 shorter events, 0.1 us)
Async XLA Ops:
  7.2 28.0 %copy-start.6 = (f32[2,64,256]{2,1,0:T(8,128)S(1)}, f32[2,64,256]{2,1,0:T(8,128)}, u32[]{:S(2)}) copy-start(f32[2,64,256]{2,1,0:T(8,128)} %param.10) | copy-start | bytes 393220
  7.2 28.0 %copy-start.7 = (f32[2,64,256]{2,1,0:T(8,128)S(1)}, f32[2,64,256]{2,1,0:T(8,128)}, u32[]{:S(2)}) copy-start(f32[2,64,256]{2,1,0:T(8,128)} %param.11) | copy-start | bytes 393220
  7.2 28.0 %copy-start.5 = (f32[2,64,256]{2,1,0:T(8,128)S(1)}, f32[2,64,256]{2,1,0:T(8,128)}, u32[]{:S(2)}) copy-start(f32[2,64,256]{2,1,0:T(8,128)} %param.9) | copy-start | bytes 393220
  7.2 69.0 %all-gather.9.cloned.1.call-start = ((), (), s32[]{:S(2)}) async-start(), calls=%async_computation.2 | async-start | bytes 1179648 | tf_op jit(solution)/shard_map/all_gather | solution.py:40
  35.2 41.0 %copy-start.3 = (bf16[48,4,2048]{2,1,0:T(4,128)(2,1)S(1)}, bf16[48,4,2048]{2,1,0:T(4,128)(2,1)}, u32[]{:S(2)}) copy-start(bf16[48,4,2048]{2,1,0:T(4,128)(2,1)} %param.13) | copy-start | bytes 2359300
  39.9 36.8 %copy-start.1 = (bf16[48,24,2,256]{3,2,1,0:T(2,128)(2,1)S(1)}, bf16[48,24,2,256]{3,2,1,0:T(2,128)(2,1)}, u32[]{:S(2)}) copy-start(bf16[48,24,2,256]{3,2,1,0:T(2,128)(2,1)} %param.14) | copy-start | bytes 3538948
  39.9 79.5 %all-gather.7.cloned.1.call-start = ((), (), s32[]{:S(2)}) async-start(), calls=%async_computation.1 | async-start | bytes 3932160 | tf_op jit(solution)/shard_map/all_gather | solution.py:113
  40.7 177.5 %all-gather.11.cloned.1.call-start = ((), (), s32[]{:S(2)}) async-start(), calls=%async_computation.3 | async-start | bytes 9437184 | tf_op jit(solution)/shard_map/all_gather | solution.py:40
  81.6 1.9 copy-start.8
  226.5 8.4 %copy-start.2 = (bf16[192,8192,1]{1,0,2:T(8,128)(2,1)S(1)}, bf16[192,8192,1]{1,0,2:T(8,128)(2,1)}, u32[]{:S(2)}) copy-start(bf16[192,8192,1]{1,0,2:T(8,128)(2,1)} %reshape.77) | copy-start | bytes 9437188
  249.7 2.2 copy-start.4
  251.9 1.8 copy-start
Sparse Core Ops, SparseCore 0:
  40.0 36.0 all-gather.8
  78.3 41.1 all-gather.6
  121.5 96.6 all-gather.10
where the time goes:
time: 262 us
  waiting for transfers between devices  164 us (63%)
  local copies, waits for them, and re-layouts  35.6 us (14%)
  blocking collectives  30.5 us (12%)
  between operations  13.9 us (5%)
  matrix products  12.7 us (5%)
  other arithmetic  5.44 us (2%)
    all_gather x2, waiting for transfers between devices, all_blocks(): parts = lax.all_gather(parts, axes[k])  129 us
    all_gather x1, waiting for transfers between devices, on_device(): gathered = lax.all_gather(layer_inputs, 'tp', axis=2, tiled=True)  34.1 us
    all_to_all x1, blocking collectives, sent_and_summed(): parts = lax.all_to_all(split_up(x, dim, size), axis, 0, 0, tiled=True)  26.7 us
    transpose x1, local copies, waits for them, and re-layouts, in_order(): return jnp.moveaxis(parts, 0, dim).reshape(dims)  8.42 us
    transpose x1, local copies, waits for them, and re-layouts, all_blocks(): parts = parts.transpose(*back, *range(len(axes), parts.ndim))  8.26 us
    reshape x1, local copies, waits for them, and re-layouts, on_device(): flattened = gathered.reshape(row_count * step_count, gathered.shape[2])  5.5 us
    dot_general x1, matrix products, on_device(): jnp.einsum('td,kdc->ktc', flattened, whole_of(rollout_weight, REP_FSDP, (...  5.27 us
  transfers between devices with their start and end apart: 3, of which 3 were waited for; matrix products, arithmetic and copies ran while one was open for 6% of the time, Pallas kernels for 0%

commit v1 on v0

--- a/solution.py
+++ b/solution.py
@@ -110,7 +110,9 @@
     rollout_weight = new_master.astype(jnp.bfloat16)
     row_count = layer_inputs.shape[0]
     step_count = layer_inputs.shape[1]
-    gathered = lax.all_gather(layer_inputs, "tp", axis=2, tiled=True)
+    gathered = jnp.concatenate(
+        lax.all_to_all(jnp.stack([layer_inputs] * lax.axis_size("tp")), "tp", 0, 0), axis=2
+    )
     flattened = gathered.reshape(row_count * step_count, gathered.shape[2])
     projected = jnp.einsum(
         "td,kdc->ktc",

time: 262 us -> 223 us (0.85)
  waiting for transfers between devices: 164 us -> 103 us
  local copies, waits for them, and re-layouts: 35.6 us -> 47.3 us
  starting transfers between devices: 0.12 us -> 9.46 us
    all_gather x2, waiting for transfers between devices: 129 us -> 75.1 us  [all_blocks(): parts = lax.all_gather(parts, axes[k])]
    all_gather x1 -> x0, waiting for transfers between devices: 34.1 us -> none  [on_device(): gathered = lax.all_gather(layer_inputs, 'tp', axis=2, tiled=True)]
    all_to_all x0 -> x1, waiting for transfers between devices: none -> 27.8 us  [on_device(): lax.all_to_all(jnp.stack([layer_inputs] * lax.axis_size('tp')), 'tp', 0, 0)]
    another operation x0 -> x2, local copies, waits for them, and re-layouts: none -> 9.48 us  [the longest x1 6.14 us: on_device(): flattened = gathered.reshape(row_count * step_count, gathered.shape[2])]
    all_to_all x0 -> x1, starting transfers between devices: none -> 9.38 us  [on_device(): lax.all_to_all(jnp.stack([layer_inputs] * lax.axis_size('tp')), 'tp', 0, 0)]
  transfers between devices with their start and end apart: 3 -> 3, of which waited for: 3 -> 3; matrix products, arithmetic and copies ran while one was open for 6% -> 11% of each run, Pallas kernels for 0% -> 0%
where the time goes in v1:
time: 223 us
  waiting for transfers between devices  103 us (46%)
  local copies, waits for them, and re-layouts  47.3 us (21%)
  blocking collectives  30.5 us (14%)
  between operations  14.2 us (6%)
  matrix products  12.7 us (6%)
  starting transfers between devices  9.46 us (4%)
  other arithmetic  5.44 us (2%)
    all_gather x2, waiting for transfers between devices, all_blocks(): parts = lax.all_gather(parts, axes[k])  75.1 us
    all_to_all x1, waiting for transfers between devices, on_device(): lax.all_to_all(jnp.stack([layer_inputs] * lax.axis_size('tp')), 'tp', 0, 0)  27.8 us
    all_to_all x1, blocking collectives, sent_and_summed(): parts = lax.all_to_all(split_up(x, dim, size), axis, 0, 0, tiled=True)  26.7 us
    all_to_all x1, starting transfers between devices, on_device(): lax.all_to_all(jnp.stack([layer_inputs] * lax.axis_size('tp')), 'tp', 0, 0)  9.38 us
    transpose x1, local copies, waits for them, and re-layouts, in_order(): return jnp.moveaxis(parts, 0, dim).reshape(dims)  8.42 us
    transpose x1, local copies, waits for them, and re-layouts, all_blocks(): parts = parts.transpose(*back, *range(len(axes), parts.ndim))  8.26 us
    reshape x1, local copies, waits for them, and re-layouts, on_device(): jnp.concatenate(lax.all_to_all(jnp.stack([layer_inputs] * lax.axis_size('...  7 us
    another operation x1, local copies, waits for them, and re-layouts, on_device(): flattened = gathered.reshape(row_count * step_count, gathered.shape[2])  6.14 us
  transfers between devices with their start and end apart: 3, of which 3 were waited for; matrix products, arithmetic and copies ran while one was open for 11% of the time, Pallas kernels for 0%

profile of v1, /device:TPU:1, one launch (start us, length us, event | category | flops | bytes accessed | tf_op | source)
XLA Modules:
  0.0 222.6 jit_solution(13188808614874497656)
XLA Ops:
  7.2 0.0 copy-start.7
  7.2 0.0 copy-start.8
  7.2 0.0 copy-start.6
  7.2 0.0 all-gather.6.cloned.1.call-start
  7.2 1.2 copy.98
  8.4 26.7 %all_to_all.10 = bf16[8,2,64,256]{3,2,1,0:T(8,128)(2,1)S(1)} all-to-all(bf16[8,2,64,256]{3,2,1,0:T(8,128)(2,1)S(1)} %copy.98), channel_id=1, replica_groups=mesh['rep_0'=8,'rep_1'=2,'fsdp'=8,'tp'=4] {'fsdp'}, dimensions={0} | all-to-all | bytes 1048576 | tf_op jit(solution)/shard_map/all_to_all | solution.py:27
  35.1 0.0 copy-start.4
  35.1 0.1 convert_reduce_fusion
  35.2 0.0 copy-done.7
  35.2 0.0 copy-done.8
  35.2 0.0 copy-done.6
  35.2 0.8 fusion.16
  36.0 3.9 %all-gather = bf16[4,64,256]{2,1,0:T(8,128)(2,1)} all-gather(bf16[2,64,256]{2,1,0:T(8,128)(2,1)S(1)} %get-tuple-element.36), channel_id=2, replica_groups=mesh['rep_0'=8,'rep_1'=2,'fsdp'=8,'tp'=4] {'rep_1'}, dimensions={0}, use_global_device_ids=true | all-gather | bytes 196608 | tf_op jit(solution)/shard_map/all_gather | solution.py:40
  39.9 0.0 all-gather.6.cloned.1.call-update
  39.9 0.0 all-gather.8.cloned.1.call-start
  39.9 36.2 %all-gather.6.cloned.1.call-done = bf16[16,2,64,256]{3,2,1,0:T(8,128)(2,1)} async-done(((bf16[2,2,64,256]{3,2,1,0:T(8,128)(2,1)}), bf16[16,2,64,256]{3,2,1,0:T(8,128)(2,1)}) %all-gather.6.cloned.1.call-update) | async-done | bytes 1048592 | tf_op jit(solution)/shard_map/all_gather | solution.py:40
  76.1 0.0 all-gather.8.cloned.1.call-update
  76.2 0.0 copy-done.4
  76.2 3.3 %stack.2 = bf16[4,48,4,2048]{3,2,1,0:T(4,128)(2,1)} broadcast(bf16[48,4,2048]{2,1,0:T(4,128)(2,1)S(1)} %copy-done.4), dimensions={1,2,3} | broadcast | bytes 3932160 | tf_op jit(solution)/shard_map/stack | solution.py:114
  79.5 0.0 copy-start.3
  79.5 9.4 %all-to-all-start.1 = ((bf16[4,48,4,2048]{3,2,1,0:T(4,128)(2,1)}), bf16[4,48,4,2048]{3,2,1,0:T(4,128)(2,1)}, u32[]{:S(2)}, u32[]{:S(2)}) async-start(bf16[4,48,4,2048]{3,2,1,0:T(4,128)(2,1)} %stack.2), calls=%async_computation.1 | async-start | bytes 6291456 | tf_op jit(solution)/shard_map/all_to_all | solution.py:114
  88.9 0.0 copy-done.3
  88.9 0.0 copy-start.1
  88.9 0.5 reshape.70
  89.4 0.8 copy-done.1
  90.2 4.9 %slice_reduce_fusion = (bf16[48,24,256]{2,1,0:T(8,128)(2,1)S(1)}, bf16[48,24,256]{2,1,0:T(8,128)(2,1)S(1)}) fusion(bf16[48,24,2,256]{3,2,1,0:T(2,128)(2,1)S(1)} %copy-done.1), kind=kLoop, calls=%fused_computation.6 | loop fusion | bytes 2359296 | tf_op jit(solution)/shard_map/slice | solution.py:66
  95.1 0.0 copy-start.9
  95.1 1.0 reshape_squeeze.6
  96.0 0.9 reshape_squeeze.7
  97.0 0.0 copy-done.9
  97.0 0.1 iota_compare_fusion
  97.1 1.7 fusion.19
  98.8 27.8 %all-to-all-done.1 = bf16[4,48,4,2048]{3,2,1,0:T(4,128)(2,1)} async-done(((bf16[4,48,4,2048]{3,2,1,0:T(4,128)(2,1)}), bf16[4,48,4,2048]{3,2,1,0:T(4,128)(2,1)}, u32[]{:S(2)}, u32[]{:S(2)}) %all-to-all-start.1) | async-done | bytes 3145760 | tf_op jit(solution)/shard_map/all_to_all | solution.py:114
  126.6 7.0 %copy.103 = bf16[48,4,4,2048]{3,2,1,0:T(4,128)(2,1)} copy(bf16[48,4,4,2048]{3,1,0,2:T(4,128)(2,1)} %bitcast.11) | data formatting | bytes 6291456 | tf_op jit(solution)/shard_map/reshape | solution.py:113
  133.6 6.1 %reshape.79 = bf16[192,8192,1]{1,0,2:T(8,128)(2,1)} reshape(bf16[48,4,4,2048]{3,2,1,0:T(4,128)(2,1)} %copy.103) | data formatting | bytes 6291456 | tf_op jit(solution)/shard_map/reshape;reshape | solution.py:116
  139.7 39.0 %all-gather.8.cloned.1.call-done = bf16[64,2,2,64,256]{4,3,2,1,0:T(8,128)(2,1)} async-done(((bf16[8,2,2,64,256]{4,3,2,1,0:T(8,128)(2,1)}), bf16[64,2,2,64,256]{4,3,2,1,0:T(8,128)(2,1)}) %all-gather.8.cloned.1.call-update) | async-done | bytes 8388624 | tf_op jit(solution)/shard_map/all_gather | solution.py:40
  178.7 8.3 %copy.101 = bf16[8,2,8,2,64,256]{5,4,3,2,1,0:T(8,128)(2,1)} copy(bf16[8,2,8,2,64,256]{5,4,3,1,0,2:T(8,128)(2,1)} %bitcast.35) | data formatting | bytes 16777216 | tf_op jit(solution)/shard_map/transpose | solution.py:43
  186.9 0.0 copy-start.2
  186.9 8.4 %copy.102 = bf16[2,128,64,256]{3,2,1,0:T(8,128)(2,1)} copy(bf16[2,128,64,256]{3,2,0,1:T(8,128)(2,1)} %bitcast.34) | data formatting | bytes 16777216 | tf_op jit(solution)/shard_map/transpose | solution.py:34
  195.3 0.0 copy-done.2
  195.3 5.3 %fusion.2 = bf16[2,192,256]{2,1,0:T(8,128)(2,1)S(1)} fusion(bf16[192,8192,1]{1,0,2:T(8,128)(2,1)S(1)} %copy-done.2, bf16[2,8192,256]{2,1,0:T(8,128)(2,1)} %bitcast.36), kind=kOutput, calls=%fused_computation.9 | convolution fusion | flops 1610711040 | bytes 11730944 | tf_op jit(solution)/shard_map/td,kdc->ktc/dot_general | solution.py:117
  200.6 0.6 fusion.18
  201.3 3.5 %fusion.6 = f32[48,2,4,4,8]{4,2,3,1,0:T(4,128)S(1)} fusion(bf16[48,4,2,8,128]{4,3,2,1,0:T(8,128)(2,1)S(1)} %reshape.70, bf16[48,4,2,128,1]{3,2,1,0,4:T(2,128)(2,1)S(1)} %bitcast.43), kind=kOutput, calls=%fused_computation.14 | convolution fusion | flops 3145728 | bytes 933888 | tf_op jit(solution)/shard_map/rsgqd,rugd->rsgqu/dot_general | solution.py:73
  204.8 0.5 copy.106
  205.3 0.7 fusion.15
  206.1 0.1 copy.108
  206.2 2.4 %copy.107 = f32[48,4,2,8,4]{4,3,1,2,0:T(8,128)S(1)} copy(f32[48,4,2,8,4]{0,3,1,4,2:T(8,128)} %get-tuple-element.35) | data formatting | bytes 98304 | tf_op jit(solution)/shard_map/jit(_where)/select_n | solution.py:83
  208.6 0.1 reduce_max.22
  208.7 1.5 fusion.11
  210.2 0.0 copy-start.5
  210.2 2.2 divide_convert_fusion
  212.4 0.0 copy-done.5
  212.4 0.0 copy-start
  212.4 1.7 fusion.4
  214.1 0.0 copy-done
  214.1 0.4 fusion.1
  214.6 0.1 copy.127
  214.7 1.1 reshape.84
  (3 shorter events, 0.1 us)
Async XLA Ops:
  7.2 28.0 %copy-start.7 = (f32[2,64,256]{2,1,0:T(8,128)S(1)}, f32[2,64,256]{2,1,0:T(8,128)}, u32[]{:S(2)}) copy-start(f32[2,64,256]{2,1,0:T(8,128)} %param.10) | copy-start | bytes 393220
  7.2 28.0 %copy-start.8 = (f32[2,64,256]{2,1,0:T(8,128)S(1)}, f32[2,64,256]{2,1,0:T(8,128)}, u32[]{:S(2)}) copy-start(f32[2,64,256]{2,1,0:T(8,128)} %param.11) | copy-start | bytes 393220
  7.2 28.0 %copy-start.6 = (f32[2,64,256]{2,1,0:T(8,128)S(1)}, f32[2,64,256]{2,1,0:T(8,128)}, u32[]{:S(2)}) copy-start(f32[2,64,256]{2,1,0:T(8,128)} %param.9) | copy-start | bytes 393220
  7.2 68.9 %all-gather.6.cloned.1.call-start = ((), (), s32[]{:S(2)}) async-start(), calls=%async_computation.2 | async-start | bytes 1179648 | tf_op jit(solution)/shard_map/all_gather | solution.py:40
  35.1 41.1 %copy-start.4 = (bf16[48,4,2048]{2,1,0:T(4,128)(2,1)S(1)}, bf16[48,4,2048]{2,1,0:T(4,128)(2,1)}, u32[]{:S(2)}) copy-start(bf16[48,4,2048]{2,1,0:T(4,128)(2,1)} %param.12) | copy-start | bytes 2359300
  39.9 138.8 %all-gather.8.cloned.1.call-start = ((), (), s32[]{:S(2)}) async-start(), calls=%async_computation.3 | async-start | bytes 9437184 | tf_op jit(solution)/shard_map/all_gather | solution.py:40
  79.5 9.4 %copy-start.3 = (bf16[48,4,2048]{2,1,0:T(4,128)(2,1)S(1)}, bf16[48,4,2048]{2,1,0:T(4,128)(2,1)}, u32[]{:S(2)}) copy-start(bf16[48,4,2048]{2,1,0:T(4,128)(2,1)} %param.13) | copy-start | bytes 2359300
  79.5 47.1 %all-to-all-start.1 = ((bf16[4,48,4,2048]{3,2,1,0:T(4,128)(2,1)}), bf16[4,48,4,2048]{3,2,1,0:T(4,128)(2,1)}, u32[]{:S(2)}, u32[]{:S(2)}) async-start(bf16[4,48,4,2048]{3,2,1,0:T(4,128)(2,1)} %stack.2), calls=%async_computation.1 | async-start | bytes 6291456 | tf_op jit(solution)/shard_map/all_to_all | solution.py:114
  88.9 1.3 copy-start.1
  95.1 1.9 copy-start.9
  186.9 8.4 %copy-start.2 = (bf16[192,8192,1]{1,0,2:T(8,128)(2,1)S(1)}, bf16[192,8192,1]{1,0,2:T(8,128)(2,1)}, u32[]{:S(2)}) copy-start(bf16[192,8192,1]{1,0,2:T(8,128)(2,1)} %reshape.79) | copy-start | bytes 9437188
  210.2 2.2 copy-start.5
  212.4 1.8 copy-start
Sparse Core Ops, SparseCore 0:
  40.0 36.0 all-gather.5
  78.2 100.4 all-gather.7
